TPU v7x, 128 devices: a whole 4x4x4 slice. The times are simulated.
128 devices in a mesh: store: 32 (over y, x, core), frame: 4 (over z).
Axes of the slice: x: 4, y: 4, z: 4, core: 2. Of those that a mesh axis runs over, the one named last changes fastest.
Arguments:
- act: bfloat16 [16384, 2048], P(('store', 'frame')), may hold values from -6 to 6
- cache_rows: bfloat16 [16384, 128], P(('store', 'frame')), may hold values from -6 to 6
- row_dest: int32 [16384], P(('store', 'frame')), may hold values from 0 to 31, as said below
- time_index: int32 [32], P('store'), may hold values from 0 to 999
- w_embed: bfloat16 [64, 2048], replicated, may hold values from -0.75 to 0.75
- norm_gain: float32 [2048], replicated, may hold values from 0.5 to 8
- w_qkv: bfloat16 [3, 2048, 2048], P(None, None, 'frame'), may hold values from -0.125 to 0.125
- w_out_attn: bfloat16 [2048, 2048], P('frame'), may hold values from -0.125 to 0.125
- w_head: bfloat16 [2048, 64], replicated, may hold values from -0.125 to 0.125
Outputs:
- frame_loss: float32 [32, 4], P('store', 'frame')
- grad_qkv: float32 [3, 2048, 2048], P(None, None, 'frame')
- grad_out_attn: float32 [2048, 2048], P('frame')
Inputs may be any that keep to these rules, and one draw needn't show every extreme that they name: `row_dest`: over the devices of one frame index, each store index is named by exactly 128 rows. The rows of one device name any one store index at most 8 times, and some store index exactly 8 times.
All inputs are finite; a program needn't handle non-finite values.
Results may differ from a plain program's by a relative error of at most 0.02.
The roundings to bfloat16 on the way count: a program that leaves them out, or rounds other values in their place, can miss the bound.
Values may be sent and summed in bfloat16 or wider, within the bound.
No kernel may reach another device: no remote copies, remote signals or barrier semaphores. Data moves between devices by JAX's collectives and lax.ppermute only.
A program may use at most 128 MiB of HBM per device.

v0:
```python
import math

import jax
import jax.numpy as jnp
from jax import lax
from jax.sharding import PartitionSpec as P

HEAD_DIM = 128
TIMESTEPS = 1000


highest = lax.Precision.HIGHEST


def shards(act, cache_rows, row_dest, time_index, w_embed, norm_gain, w_qkv, w_out_attn, w_head):
    f32 = jnp.float32
    bf16 = jnp.bfloat16
    store_count = lax.axis_size("store")
    frame_count = lax.axis_size("frame")
    frame_rows = act.shape[0]
    capacity = max(2, 2 * frame_rows // store_count)
    columns = cache_rows.shape[1]
    patch_width = w_head.shape[1]
    dest_onehot = (row_dest[:, None] == jnp.arange(store_count, dtype=jnp.int32)[None, :]).astype(
        jnp.int32
    )
    earlier = jnp.cumsum(dest_onehot, axis=0) - dest_onehot
    position = jnp.sum(earlier * dest_onehot, axis=1)
    bucket_slot = row_dest * capacity + position
    outgoing = jnp.zeros((store_count * capacity, columns), bf16).at[bucket_slot].set(cache_rows)
    outgoing = outgoing.reshape(store_count, capacity, columns)
    tallies_out = jnp.sum(dest_onehot, axis=0).astype(bf16).reshape(store_count, 1)
    arrived, tallies_in = (
        lax.all_to_all(outgoing, "store", split_axis=0, concat_axis=0, tiled=True),
        lax.all_to_all(tallies_out, "store", split_axis=0, concat_axis=0, tiled=True),
    )
    tallies = tallies_in[:, 0].astype(jnp.int32)
    starting = jnp.cumsum(tallies) - tallies
    within = jnp.arange(capacity, dtype=jnp.int32)[None, :]
    landing = jnp.where(within < tallies[:, None], starting[:, None] + within, frame_rows).reshape(
        -1
    )
    fetched = (
        jnp.zeros((frame_rows, columns), bf16)
        .at[landing]
        .set(arrived.reshape(store_count * capacity, columns), mode="drop")
    )
    moment = (time_index[0].astype(f32) + 0.5) / TIMESTEPS
    noise = fetched[:, :patch_width].astype(f32)
    endpoint = fetched[:, patch_width:].astype(f32)
    noised = ((1.0 - moment) * noise + moment * endpoint).astype(bf16)
    velocity = endpoint - noise
    hidden = act.astype(f32) + jnp.dot(noised, w_embed, preferred_element_type=f32)
    normed = (
        hidden * lax.rsqrt(jnp.mean(hidden * hidden, axis=1, keepdims=True) + 1e-06) * norm_gain
    ).astype(bf16)
    normed_all = lax.all_gather(normed, "frame", axis=0, tiled=True)
    head_cols = w_qkv.shape[2]
    head_count = head_cols // HEAD_DIM
    rows_all = frame_count * frame_rows
    joined = jnp.concatenate([w_qkv[0], w_qkv[1], w_qkv[2]], axis=1)
    projected = jnp.dot(normed_all, joined, preferred_element_type=f32).astype(bf16)
    shape4 = (frame_count, frame_rows, head_count, HEAD_DIM)
    query_b = projected[:, :head_cols].reshape(shape4)
    key_b = projected[:, head_cols : 2 * head_cols].reshape(shape4)
    value_b = projected[:, 2 * head_cols :].reshape(shape4)
    inv_root = 1.0 / math.sqrt(HEAD_DIM)
    scores = jnp.einsum("fphd,gphd->phfg", query_b, key_b, preferred_element_type=f32) * inv_root
    probs = jax.nn.softmax(scores, axis=-1)
    probs_b = probs.astype(bf16)
    attended = jnp.einsum("phfg,gphd->fphd", probs_b, value_b, preferred_element_type=f32).astype(
        bf16
    )
    attended = attended.reshape(rows_all, head_cols)
    head_f32 = w_head.astype(f32)
    contraction = (((0,), (0,)), ((), ()))
    att_rows = attended
    block_out = hidden + lax.psum_scatter(
        jnp.dot(att_rows, w_out_attn, preferred_element_type=f32),
        "frame",
        scatter_dimension=0,
        tiled=True,
    )
    predicted = jnp.dot(block_out, head_f32, precision=highest)
    error = predicted - velocity
    frame_loss = jnp.mean(error * error).reshape(1, 1)
    slope = 2.0 * error / store_count
    upstream = jnp.dot(slope, head_f32.T, precision=highest).astype(bf16)
    upstream_rows = lax.all_gather(upstream, "frame", axis=0, tiled=True)
    grad_rows = jnp.dot(upstream_rows, w_out_attn.T, preferred_element_type=f32)
    att_rows = attended
    inner = lax.dot_general(att_rows, upstream_rows, contraction, preferred_element_type=f32)
    query_f = query_b.astype(f32)
    key_f = key_b.astype(f32)
    value_f = value_b.astype(f32)
    probs_f = lax.optimization_barrier(probs_b).astype(f32)
    grad4 = grad_rows.reshape(shape4)
    dprob = jnp.einsum("fphd,gphd->phfg", grad4, value_f)
    dvalue = jnp.einsum("phfg,fphd->gphd", probs_f, grad4)
    dscore = probs * (dprob - jnp.sum(dprob * probs, axis=-1, keepdims=True))
    dquery = jnp.einsum("phfg,gphd->fphd", dscore, key_f) * inv_root
    dkey = jnp.einsum("phfg,fphd->gphd", dscore, query_f) * inv_root
    pieces = []
    for derivative in (dquery, dkey, dvalue):
        flat = derivative.astype(bf16).reshape(rows_all, head_cols)
        pieces.append(lax.dot_general(normed_all, flat, contraction, preferred_element_type=f32))
    grad_stack = jnp.stack(pieces)
    grad_qkv, grad_out_attn = (
        lax.psum(grad_stack.astype(jnp.bfloat16), "store").astype(jnp.float32),
        lax.psum(inner.astype(jnp.bfloat16), "store").astype(jnp.float32),
    )
    return (frame_loss, grad_qkv, grad_out_attn)


def solution(mesh):
    in_specs = (
        P(("store", "frame"), None),
        P(("store", "frame"), None),
        P(("store", "frame")),
        P("store"),
        P(),
        P(),
        P(None, None, "frame"),
        P("frame", None),
        P(),
    )
    out_specs = (P("store", "frame"), P(None, None, "frame"), P("frame", None))
    return jax.shard_map(shards, mesh=mesh, in_specs=in_specs, out_specs=out_specs, check_vma=False)
```

profile of v0, /device:TPU:1, one launch (start us, length us, event | category | flops | bytes accessed | tf_op | source)
XLA Modules:
  0.0 341.2 jit_solution(8643710492589661916)
XLA Ops:
  7.2 0.9 fusion.44
  8.3 0.8 select_reduce_fusion
  9.1 0.7 copy.58
  9.8 8.6 %all-to-all-start = ((bf16[32,1,1]{2,1,0:T(2,128)(2,1)}), bf16[32,1,1]{2,1,0:T(2,128)(2,1)S(1)}, u32[]{:S(2)}, u32[]{:S(2)}) async-start(bf16[32,1,1]{2,1,0:T(2,128)(2,1)} %copy.58), calls=%async_computation | async-start | bytes 32768 | tf_op jit(solution)/shard_map/all_to_all | solution.py:35
  18.4 0.7 compare_select_fusion.1
  19.7 1.7 scatter_custom_fusion
  21.4 3.8 %all-to-all-done = bf16[32,1,1]{2,1,0:T(2,128)(2,1)S(1)} async-done(((bf16[32,1,1]{2,1,0:T(2,128)(2,1)}), bf16[32,1,1]{2,1,0:T(2,128)(2,1)S(1)}, u32[]{:S(2)}, u32[]{:S(2)}) %all-to-all-start) | async-done | bytes 96 | tf_op jit(solution)/shard_map/all_to_all | solution.py:35
  25.3 4.2 %all-to-all-start.1 = ((bf16[32,8,128]{2,1,0:T(8,128)(2,1)}), bf16[32,8,128]{2,1,0:T(8,128)(2,1)S(1)}, u32[]{:S(2)}, u32[]{:S(2)}) async-start(bf16[32,8,128]{2,1,0:T(8,128)(2,1)} %bitcast.4), calls=%async_computation.1 | async-start | bytes 131072 | tf_op jit(solution)/shard_map/all_to_all | solution.py:34
  29.7 0.7 convert_reduce_fusion
  30.6 6.3 %all-to-all-done.1 = bf16[32,8,128]{2,1,0:T(8,128)(2,1)S(1)} async-done(((bf16[32,8,128]{2,1,0:T(8,128)(2,1)}), bf16[32,8,128]{2,1,0:T(8,128)(2,1)S(1)}, u32[]{:S(2)}, u32[]{:S(2)}) %all-to-all-start.1) | async-done | bytes 65568 | tf_op jit(solution)/shard_map/all_to_all | solution.py:34
  36.9 1.2 scatter_custom_fusion.1
  38.3 1.6 multiply_reduce_fusion.1
  39.9 0.9 multiply_convert_fusion
  40.9 5.7 %slice_bitcast_fusion.2 = (bf16[2048,512]{1,0:T(8,128)(2,1)}, bf16[2048,512]{1,0:T(8,128)(2,1)}, bf16[2048,512]{1,0:T(8,128)(2,1)}) fusion(bf16[3,2048,512]{2,1,0:T(8,128)(2,1)} %param.15), kind=kLoop, calls=%fused_computation.22 | loop fusion | bytes 12582912 | tf_op jit(solution)/shard_map/squeeze | solution.py:61
  46.6 23.9 %all-gather.3.cloned.1.call-done = bf16[512,2048]{1,0:T(8,128)(2,1)} async-done(((bf16[128,2048]{1,0:T(8,128)(2,1)}), bf16[512,2048]{1,0:T(8,128)(2,1)}) %all-gather.3.cloned.1.call-update) | async-done | bytes 2097168 | tf_op jit(solution)/shard_map/all_gather | solution.py:57
  70.5 6.9 %fusion.7 = bf16[512,1536]{1,0:T(8,128)(2,1)S(1)} fusion(bf16[512,2048]{1,0:T(8,128)(2,1)} %all-gather.3.cloned.1.call-done, bf16[2048,512]{1,0:T(8,128)(2,1)} %get-tuple-element.8, bf16[2048,512]{1,0:T(8,128)(2,1)} %get-tuple-element.9, bf16[2048,512]{1,0:T(8,128)(2,1)} %get-tuple-element.7), kind=kOutput, calls=%fused_computation.10 | convolution fusion | flops 3240886272 | bytes 9961472 | tf_op jit(solution)/shard_map/dot_general | solution.py:62
  77.3 1.2 fusion.59
  78.5 2.0 reshape.164
  80.5 2.0 reshape.163
  82.5 2.0 reshape.162
  84.4 4.1 %fusion.61 = (f32[128,4,4]{2,1,0:T(4,128)S(1)}, f32[128,4,4,4]{2,3,1,0:T(4,128)}) fusion(bf16[4,128,4,128]{3,2,1,0:T(4,128)(2,1)} %reshape.164, bf16[4,128,4,128]{3,2,1,0:T(4,128)(2,1)} %reshape.163), kind=kOutput, calls=%fused_computation.94 | convolution fusion | flops 2121731 | bytes 1089536 | tf_op jit(solution)/shard_map/sub | solution.py:69
  88.5 1.6 fusion.58
  90.2 0.8 copy-done.7
  91.0 1.8 fusion.20
  92.8 0.2 copy.66
  93.0 0.8 copy-done.3
  93.8 3.3 fusion.32
  97.2 0.2 all-gather.5.cloned.1.call-start
  97.4 46.9 %reduce-scatter.2.cloned.1.call-done = f32[128,2048]{1,0:T(8,128)} async-done(((f32[512,2048]{1,0:T(8,128)}), f32[128,2048]{1,0:T(8,128)}) %reduce-scatter.2.cloned.1.call-update) | async-done | bytes 1048592 | tf_op jit(solution)/shard_map/reduce_scatter | solution.py:78
  144.3 2.6 multiply_reduce_fusion.2
  146.8 1.4 convolution_convert_fusion.4
  148.4 30.7 %all-gather.5.cloned.1.call-done = bf16[512,2048]{1,0:T(8,128)(2,1)} async-done(((bf16[128,2048]{1,0:T(8,128)(2,1)}), bf16[512,2048]{1,0:T(8,128)(2,1)}) %all-gather.5.cloned.1.call-update) | async-done | bytes 2097168 | tf_op jit(solution)/shard_map/all_gather | solution.py:89
  179.0 3.7 %fusion.66 = bf16[512,512]{1,0:T(8,128)(2,1)} fusion(bf16[512,2048]{1,0:T(8,128)(2,1)} %all-gather.5.cloned.1.call-done, bf16[512,2048]{1,0:T(8,128)(2,1)S(1)} %copy-done), kind=kOutput, calls=%fused_computation.95 | convolution fusion | flops 1073741824 | bytes 4718592 | tf_op jit(solution)/shard_map/dot_general | solution.py:90
  182.7 1.2 reshape.167
  183.9 2.6 multiply_reduce_fusion
  186.5 1.1 fusion.18
  187.6 1.1 fusion.19
  188.7 0.7 fusion.17
  189.4 0.2 copy.75
  190.1 0.9 copy-done.14
  191.0 1.3 fusion.12
  192.3 1.3 fusion.11
  193.6 1.3 fusion.10
  195.0 3.3 pad_maximum_fusion
  198.3 2.6 convolution_convert_fusion
  201.6 119.9 %all-reduce.3.cloned.1.call-done = (bf16[3,2048,512]{2,1,0:T(8,128)(2,1)}, bf16[512,2048]{1,0:T(8,128)(2,1)}) async-done(((bf16[3,2048,512]{2,1,0:T(8,128)(2,1)}, bf16[512,2048]{1,0:T(8,128)(2,1)}), (bf16[3,2048,512]{2,1,0:T(8,128)(2,1)}, bf16[512,2048]{1,0:T(8,128)(2,1)})) %all-reduce.3.cloned.1.call-update) | async-done | bytes 8388624 | tf_op jit(solution)/shard_map/psum | solution.py:109
  321.5 9.5 %convert_element_type.131 = f32[3,2048,512]{2,1,0:T(8,128)} convert(bf16[3,2048,512]{2,1,0:T(8,128)(2,1)} %get-tuple-element.5) | non-fusion elementwise | flops 3145728 | bytes 18874368 | tf_op jit(solution)/shard_map/convert_element_type | solution.py:109
  331.0 2.5 convert_element_type.133
  (51 shorter events, 1.5 us)
Async XLA Ops:
  7.2 86.7 %copy-start = (bf16[512,2048]{1,0:T(8,128)(2,1)S(1)}, bf16[512,2048]{1,0:T(8,128)(2,1)}, u32[]{:S(2)}) copy-start(bf16[512,2048]{1,0:T(8,128)(2,1)} %param.16) | copy-start | bytes 6291460
  7.2 32.7 %copy-start.13 = (f32[2048]{0:T(1024)S(1)}, f32[2048]{0:T(1024)}, u32[]{:S(2)}) copy-start(f32[2048]{0:T(1024)} %param.14) | copy-start | bytes 24580
  9.8 15.5 %all-to-all-start = ((bf16[32,1,1]{2,1,0:T(2,128)(2,1)}), bf16[32,1,1]{2,1,0:T(2,128)(2,1)S(1)}, u32[]{:S(2)}, u32[]{:S(2)}) async-start(bf16[32,1,1]{2,1,0:T(2,128)(2,1)} %copy.58), calls=%async_computation | async-start | bytes 32768 | tf_op jit(solution)/shard_map/all_to_all | solution.py:35
  25.3 11.6 %all-to-all-start.1 = ((bf16[32,8,128]{2,1,0:T(8,128)(2,1)}), bf16[32,8,128]{2,1,0:T(8,128)(2,1)S(1)}, u32[]{:S(2)}, u32[]{:S(2)}) async-start(bf16[32,8,128]{2,1,0:T(8,128)(2,1)} %bitcast.4), calls=%async_computation.1 | async-start | bytes 131072 | tf_op jit(solution)/shard_map/all_to_all | solution.py:34
  29.4 41.0 %all-gather.3.cloned.1.call-start = ((), (), s32[]{:S(2)}) async-start(), calls=%async_computation.3 | async-start | bytes 2621440 | tf_op jit(solution)/shard_map/all_gather | solution.py:57
  40.9 103.4 %reduce-scatter.2.cloned.1.call-start = ((), (), s32[]{:S(2)}) async-start(), calls=%async_computation.4 | async-start | bytes 5242880 | tf_op jit(solution)/shard_map/reduce_scatter | solution.py:78
  88.5 4.5 %copy-start.11 = (f32[128,4,4]{2,1,0:T(4,128)}, f32[128,4,4]{2,1,0:T(4,128)S(1)}, u32[]{:S(2)}) copy-start(f32[128,4,4]{2,1,0:T(4,128)S(1)} %get-tuple-element.17) | copy-start | bytes 24580
  90.2 0.8 copy-start.7
  93.0 0.8 copy-start.3
  97.1 47.1 %copy-start.6 = (bf16[2048,64]{0,1:T(8,128)(2,1)S(1)}, bf16[2048,64]{0,1:T(8,128)(2,1)}, u32[]{:S(2)}) copy-start(bf16[2048,64]{0,1:T(8,128)(2,1)} %param.17) | copy-start | bytes 786436
  97.2 81.9 %all-gather.5.cloned.1.call-start = ((), (), s32[]{:S(2)}) async-start(), calls=%async_computation.5 | async-start | bytes 2621440 | tf_op jit(solution)/shard_map/all_gather | solution.py:89
  148.3 35.6 %copy-start.5 = (f32[128,4,4,4]{2,3,1,0:T(4,128)S(1)}, f32[128,4,4,4]{2,3,1,0:T(4,128)}, u32[]{:S(2)}) copy-start(f32[128,4,4,4]{2,3,1,0:T(4,128)} %get-tuple-element.18) | copy-start | bytes 98308
  148.3 35.6 %copy-start.12 = (f32[128,4,4]{2,1,0:T(4,128)S(1)}, f32[128,4,4]{2,1,0:T(4,128)}, u32[]{:S(2)}) copy-start(f32[128,4,4]{2,1,0:T(4,128)} %copy-done.11) | copy-start | bytes 24580
  148.3 173.2 %all-reduce.3.cloned.1.call-start = ((), (), s32[]{:S(2)}) async-start(), calls=%async_computation.6 | async-start | bytes 16777216 | tf_op jit(solution)/shard_map/psum | solution.py:109
  183.9 2.6 copy-start.10
  186.5 1.1 copy-start.9
  187.6 1.2 copy-start.8
  189.4 1.6 copy-start.14
  195.0 3.4 copy-start.4
  195.0 3.4 copy-start.15
  321.5 9.5 %copy-start.2 = (bf16[512,2048]{1,0:T(8,128)(2,1)S(1)}, bf16[512,2048]{1,0:T(8,128)(2,1)}, u32[]{:S(2)}) copy-start(bf16[512,2048]{1,0:T(8,128)(2,1)} %get-tuple-element.6) | copy-start | bytes 6291460
  331.0 2.5 copy-start.1
Sparse Core Ops, SparseCore 0:
  41.0 29.4 all-gather.2
  97.3 46.9 reduce-scatter.1
  148.4 30.5 all-gather.4
  201.1 120.3 all-reduce.2
where the time goes:
time: 342 us; the launch traced here: 341 us
  waiting for transfers between devices  232 us (68%)
  matrix products  37.3 us (11%)
  other arithmetic  21.5 us (6%)
  local copies, waits for them, and re-layouts  21.3 us (6%)
  between operations  16.6 us (5%)
  starting transfers between devices  13.1 us (4%)
    psum x1, waiting for transfers between devices, shards(): lax.psum(grad_stack.astype(jnp.bfloat16), 'store').astype(jnp.float32)  120 us
    reduce_scatter x1, waiting for transfers between devices, shards(): lax.psum_scatter(jnp.dot(att_rows, w_out_attn, preferred_element_type=f32...  46.9 us
    all_gather x1, waiting for transfers between devices, shards(): upstream_rows = lax.all_gather(upstream, 'frame', axis=0, tiled=True)  30.7 us
    all_gather x1, waiting for transfers between devices, shards(): normed_all = lax.all_gather(normed, 'frame', axis=0, tiled=True)  23.9 us
    convert_element_type x1, other arithmetic, shards(): lax.psum(grad_stack.astype(jnp.bfloat16), 'store').astype(jnp.float32)  9.52 us
    all_to_all x1, starting transfers between devices, shards(): lax.all_to_all(tallies_out, 'store', split_axis=0, concat_axis=0, tiled=T...  8.59 us
    dot_general x1, matrix products, shards(): jnp.dot(normed_all, joined, preferred_element_type=f32).astype(bf16)  6.87 us
  transfers between devices with their start and end apart: 6, of which 6 were waited for; matrix products, arithmetic and copies ran while one was open for 3% of the time, Pallas kernels for 0%

commit v1 on v0

v1 whole, which is shorter than its diff:
```python
import functools
import math

import jax
import jax.numpy as jnp
from jax import lax
from jax.experimental import pallas as pl
from jax.experimental.pallas import tpu as pltpu
from jax.sharding import Mesh, PartitionSpec as P

HEAD_DIM = 128
TIMESTEPS = 1000
UNUSED = 64.0
f32 = jnp.float32
bf16 = jnp.bfloat16
HIGHEST = lax.Precision.HIGHEST
INV_ROOT = 1.0 / math.sqrt(HEAD_DIM)
NN = (((1,), (0,)), ((), ()))
NT = (((1,), (1,)), ((), ()))
TN = (((0,), (0,)), ((), ()))
ORDER = (0, 1, 3, 2)
SPOT = {r: i for i, r in enumerate(ORDER)}
VMEM = pl.BlockSpec(memory_space=pltpu.VMEM)
SMEM = pl.BlockSpec(memory_space=pltpu.SMEM)


def params(mib):
    return pltpu.CompilerParams(vmem_limit_bytes=mib << 20)


def cost(flops, moved):
    return pl.CostEstimate(flops=flops, bytes_accessed=moved, transcendentals=0)


def dot(a, b, dims=NN, precision=None):
    return lax.dot_general(a, b, dims, preferred_element_type=f32, precision=precision)


def shift(value, axis, offset):
    size = lax.axis_size(axis)
    return lax.ppermute(value, axis, [(i, (i + offset) % size) for i in range(size)])


def shape(dims, kind):
    return jax.ShapeDtypeStruct(dims, kind)


def bucket_kernel(rows, dest_row, dest_col, out):
    earlier = lax.broadcasted_iota(jnp.int32, (128, 128), 0) < lax.broadcasted_iota(
        jnp.int32, (128, 128), 1
    )
    same = jnp.where((dest_col[...] == dest_row[...]) & earlier, 1.0, 0.0)
    slot = dest_row[...] * 8 + jnp.sum(same, axis=0, keepdims=True).astype(jnp.int32)
    hot = jnp.where(lax.broadcasted_iota(jnp.int32, (256, 128), 0) == slot, 1.0, 0.0)
    used = jnp.max(hot, axis=1, keepdims=True)
    moved = dot(hot.astype(bf16), rows[...]) + (1.0 - used) * UNUSED
    bucket = moved.astype(bf16).reshape(16, 16, 128)
    for frame in range(4):
        for core in range(2):
            out[frame, :, core] = bucket


def prepare_kernel(place, w, w_out, head_t, w_t, mix, mix_t):
    for h in range(2):
        w_t[h, 0] = w[0, :, h * 128 : h * 128 + 128].T

    @pl.when(pl.program_id(0) == 0)
    def _():
        mix[...] = dot(w_out[...], head_t[...], NT)
        mix_t[...] = dot(head_t[...], w_out[...], NT)


def fetch_kernel(place, arrived, pairs):
    frame, core = place[0], place[1]
    slots = 512
    before = jnp.where(
        lax.broadcasted_iota(jnp.int32, (slots, slots), 1)
        < lax.broadcasted_iota(jnp.int32, (slots, slots), 0),
        1.0,
        0.0,
    ).astype(bf16)
    half = (lax.broadcasted_iota(jnp.int32, (slots, 128), 0) // 8) % 2
    lane = lax.broadcasted_iota(jnp.int32, (slots, 128), 1).astype(f32)
    for i, r in enumerate(ORDER):
        rows = arrived[(frame + 4 - r) % 4]
        valid = jnp.broadcast_to(rows[:, 0:1].astype(f32), (slots, 128)) < 32.0
        for other in range(2):
            clip = core + other - 2 * core * other
            mine = jnp.where(valid & (half == clip), 1.0, 0.0)
            rank = dot(before, mine.astype(bf16))
            pick = jnp.where(rank == lane, mine, 0.0)
            pairs[2 * i + other] = dot(pick.astype(bf16), rows, TN).astype(bf16)


def embed_kernel(first, count, moments, *refs):
    acts, refs = refs[:count], refs[count:]
    pairs, w_embed, gain, w_t, head_t = refs[:5]
    normed, proj = refs[5:7]
    for b in range(count):
        pair = pairs[first + b].astype(f32)
        t = moments[b % 2]
        noised = ((1.0 - t) * pair[:, :64] + t * pair[:, 64:]).astype(bf16)
        hidden = acts[b][...].astype(f32) + dot(noised, w_embed[...])
        scale = lax.rsqrt(jnp.mean(hidden * hidden, axis=1, keepdims=True) + 1e-06)
        normed[b * 128 : b * 128 + 128] = (hidden * scale * gain[...]).astype(bf16)
        if first + b == 0:
            turned = pair.T
            rest = dot(head_t[...].astype(f32), hidden, NT, HIGHEST)
            refs[7][...] = rest - (turned[64:] - turned[:64])
    for i in range(3):
        rows = slice(i * 256, i * 256 + 256)
        proj[rows] = dot(w_t[rows], normed[...], NT).astype(bf16)


def part_of(proj_a, proj_b, row, i, other):
    ref, column = (proj_a, 2 * i + other) if i < 3 else (proj_b, other)
    return ref[row : row + 128, column * 128 : column * 128 + 128].astype(f32)


def lanes(i, other):
    return slice((2 * i + other) * 128, (2 * i + other) * 128 + 128)


def attend_kernel(proj_a, proj_b, mix_t, rest, attended, probs, part_own, part_other):
    for h in range(2):
        for other in range(2):
            read = functools.partial(part_of, proj_a, proj_b)
            keys = [read(h * 384 + 128, g, other) for g in range(4)]
            values = [read(h * 384 + 256, g, other) for g in range(4)]
            for f in range(4):
                query = read(h * 384, f, other)
                scores = [jnp.sum(query * k, axis=0, keepdims=True) * INV_ROOT for k in keys]
                top = jnp.maximum(jnp.maximum(scores[0], scores[1]), jnp.maximum(scores[2], scores[3]))
                powers = [jnp.exp(s - top) for s in scores]
                whole = powers[0] + powers[1] + powers[2] + powers[3]
                prob = [p / whole for p in powers]
                rounded = [p.astype(bf16).astype(f32) for p in prob]
                out = rounded[0] * values[0]
                for g in range(1, 4):
                    out = out + rounded[g] * values[g]
                attended[h * 128 : h * 128 + 128, lanes(f, other)] = out.astype(bf16)
                for g in range(4):
                    probs[h * 2 + other, f * 4 + g : f * 4 + g + 1] = prob[g]
    for other, part in ((0, part_own), (1, part_other)):
        for f in range(4):
            here = attended[:, lanes(f, other)].astype(f32)
            value = dot(mix_t[...], here, NN, HIGHEST)
            if other == 0 and f == 0:
                value = value + rest[...]
            part[:, f * 128 : f * 128 + 128] = value


def gradient_piece(delta, normed_a, normed_b, h, block):
    columns = pl.ds(pl.multiple_of(block * 512, 512), 512)
    rows = slice(h * 384, h * 384 + 384)
    return (
        dot(delta[rows, :768], normed_a[:, columns]) + dot(delta[rows, 768:], normed_b[:, columns])
    ).astype(bf16)


def backward_kernel(
    place, error_own, error_other, proj_a, proj_b, normed_a, normed_b, probs, attended, mix, *refs
):
    pieces, delta, own_factor = refs[:6], refs[6], refs[7]
    slope, grad = refs[8:]
    for i in range(4):
        for other, error in ((0, error_own), (1, error_other)):
            slope[:, lanes(i, other)] = error[:, i * 128 : i * 128 + 128] * (2.0 / 32.0)
    grad[...] = dot(mix[...], slope[...], NN, HIGHEST)
    for h in range(2):
        for other in range(2):
            read = functools.partial(part_of, proj_a, proj_b)
            grads = [grad[h * 128 : h * 128 + 128, lanes(f, other)] for f in range(4)]
            score = [[None] * 4 for _ in range(4)]
            for f in range(4):
                prob = [probs[h * 2 + other, f * 4 + g : f * 4 + g + 1] for g in range(4)]
                dprob = [
                    jnp.sum(grads[f] * read(h * 384 + 256, g, other), axis=0, keepdims=True)
                    for g in range(4)
                ]
                mean = sum(d * p for d, p in zip(dprob, prob))
                for g in range(4):
                    score[f][g] = prob[g] * (dprob[g] - mean) * INV_ROOT
            for g in range(4):
                value = sum(
                    probs[h * 2 + other, f * 4 + g : f * 4 + g + 1].astype(bf16).astype(f32) * grads[f]
                    for f in range(4)
                )
                query = sum(score[g][i] * read(h * 384 + 128, i, other) for i in range(4))
                key = sum(score[f][g] * read(h * 384, f, other) for f in range(4))
                for j, out in enumerate((query, key, value)):
                    row = h * 384 + j * 128
                    delta[row : row + 128, lanes(g, other)] = out.astype(bf16)
    for h in range(2):
        factor = dot(slope[...], attended[h * 128 : h * 128 + 128].astype(f32), NT, HIGHEST)
        factor = factor.astype(bf16)
        own_factor[h] = factor
        for k, o in enumerate((1, 3, 2)):
            out = pieces[h * 3 + k]
            out[:384] = gradient_piece(delta, normed_a, normed_b, h, (place[h] + o) % 4)
            for i in range(4):
                out[384:, i * 128 : i * 128 + 128] = factor[i * 16 : i * 16 + 16]


def keep_kernel(place, delta, normed_a, normed_b, own_factor, out_x, out_y):
    for h, out in ((0, out_x), (1, out_y)):
        out[:384] = gradient_piece(delta, normed_a, normed_b, h, place[h])
        for i in range(4):
            out[384:, i * 128 : i * 128 + 128] = own_factor[h, i * 16 : i * 16 + 16]


def add_first_kernel(place, *refs):
    parts, outs, both = refs[:4], refs[4:8], refs[8]
    total = parts[0][...].astype(f32)
    for part in parts[1:]:
        total = total + part[...].astype(f32)
    both[...] = total.astype(bf16)
    for o, out in enumerate(outs):
        columns = pl.ds(pl.multiple_of(((place[0] + o) % 4) * 128, 128), 128)
        out[:384] = both[:384, columns]
        for i in range(4):
            out[384 + i * 16 : 400 + i * 16] = both[384:, i * 128 : i * 128 + 128]


def add_second_kernel(*refs):
    parts, owned, factor = refs[:4], refs[4], refs[5]
    total = parts[0][...].astype(f32)
    for part in parts[1:]:
        total = total + part[...].astype(f32)
    for j in range(3):
        owned[j] = total[j * 128 : j * 128 + 128].T.astype(bf16)
    factor[...] = total[384:].T.astype(bf16)


def assemble_kernel(chosen, aliased, place, *refs):
    count = len(chosen) * 4
    pieces, out = refs[:count], refs[count + aliased]
    held, ready, done, sems = refs[count + aliased + 1 :]
    loads = [pltpu.make_async_copy(p, held.at[k], sems.at[k]) for k, p in enumerate(pieces)]
    for load in loads:
        load.start()
    stores = [None, None]
    for k in range(count):
        o, theirs, h = chosen[k // 4], (k // 2) % 2, k % 2
        slot = k % 2
        loads[k].wait()
        if stores[slot] is not None:
            stores[slot].wait()
        first = (place[h] + 4 - o) % 4
        for inner in range(4):
            second = (place[1 - h] + 4 - inner) % 4
            ready[slot, :, pl.ds(pl.multiple_of(second * 128, 128), 128)] = held[k, inner].astype(f32)
        core = place[2] if theirs == 0 else 1 - place[2]
        stores[slot] = pltpu.make_async_copy(
            ready.at[slot],
            out.at[
                :,
                pl.ds(pl.multiple_of(first * 512, 512), 512),
                pl.ds(pl.multiple_of(core * 256 + h * 128, 128), 128),
            ],
            done.at[slot],
        )
        stores[slot].start()
    for store in stores:
        store.wait()


def assemble(place, pieces, chosen, onto=None):
    count = len(chosen) * 4
    anywhere = pl.BlockSpec(memory_space=pl.ANY)
    given = [] if onto is None else [onto]
    return pl.pallas_call(
        functools.partial(assemble_kernel, chosen, len(given)),
        in_specs=[SMEM] + [anywhere] * (count + len(given)),
        out_specs=anywhere,
        out_shape=shape((3, 2048, 512), f32),
        scratch_shapes=[
            pltpu.VMEM((count, 4, 3, 128, 128), bf16),
            pltpu.VMEM((2, 3, 512, 128), f32),
            pltpu.SemaphoreType.DMA((2,)),
            pltpu.SemaphoreType.DMA((count,)),
        ],
        input_output_aliases={1 + count: 0} if given else {},
        compiler_params=params(16),
        cost_estimate=cost(0, count * 3 * 393216),
    )(place, *pieces, *given)


def shards(act, cache_rows, row_dest, time_index, w_embed, norm_gain, w_qkv, w_out, w_head):
    x, y, core, frame = (lax.axis_index(a).astype(jnp.int32) for a in ("x", "y", "core", "frame"))
    here = jnp.stack([frame, core])
    square = jnp.stack([x, y, core])

    act_by = {0: act, **{o: shift(act, "frame", o) for o in (1, 3, 2)}}
    act_other = {r: shift(act_by[r], "core", 1) for r in ORDER}

    sent = pl.pallas_call(
        bucket_kernel,
        in_specs=[VMEM] * 3,
        out_specs=VMEM,
        out_shape=shape((4, 16, 2, 16, 128), bf16),
    )(cache_rows, row_dest.reshape(1, 128), row_dest.reshape(128, 1))
    arrived = lax.all_to_all(
        sent.reshape(128, 16, 128), ("frame", "y", "x", "core"), 0, 0, tiled=True
    ).reshape(4, 512, 128)
    moment = (time_index.astype(f32) + 0.5) / TIMESTEPS
    moments = jnp.concatenate([moment, shift(moment, "core", 1)])

    head_t = w_head.T
    w_t, mix, mix_t = pl.pallas_call(
        prepare_kernel,
        grid_spec=pltpu.PrefetchScalarGridSpec(
            num_scalar_prefetch=1,
            grid=(3,),
            in_specs=[
                pl.BlockSpec((1, 2048, 256), lambda j, p: (j, 0, p[1])),
                pl.BlockSpec((256, 2048), lambda j, p: (p[1], 0)),
                pl.BlockSpec((64, 2048), lambda j, p: (0, 0)),
            ],
            out_specs=[
                pl.BlockSpec((2, 1, 128, 2048), lambda j, p: (0, j, 0, 0)),
                pl.BlockSpec((256, 64), lambda j, p: (0, 0)),
                pl.BlockSpec((64, 256), lambda j, p: (0, 0)),
            ],
        ),
        out_shape=[shape((2, 3, 128, 2048), bf16), shape((256, 64), f32), shape((64, 256), f32)],
        compiler_params=params(20),
        cost_estimate=cost(2 * 2 * 256 * 2048 * 64, 8 << 20),
    )(here, w_qkv, w_out, head_t)
    w_t = w_t.reshape(768, 2048)

    pairs = pl.pallas_call(
        fetch_kernel,
        in_specs=[SMEM, VMEM],
        out_specs=VMEM,
        out_shape=shape((8, 128, 128), bf16),
        compiler_params=params(12),
        cost_estimate=cost(600_000_000, 1 << 20),
    )(here, arrived)

    def embed(first, order):
        blocks = [a for r in order for a in (act_by[r], act_other[r])]
        count = len(blocks)
        out = [shape((count * 128, 2048), bf16), shape((768, count * 128), bf16)]
        if first == 0:
            out.append(shape((64, 128), f32))
        return pl.pallas_call(
            functools.partial(embed_kernel, first, count),
            in_specs=[SMEM] + [VMEM] * (count + 5),
            out_specs=[VMEM] * len(out),
            out_shape=out,
            compiler_params=params(40),
            cost_estimate=cost(count * 128 * 2048 * 768 * 2, count * (1 << 20) + (3 << 20)),
        )(moments, *blocks, pairs, w_embed, norm_gain.reshape(1, 2048), w_t, head_t)

    normed_a, proj_a, rest = embed(0, ORDER[:3])
    normed_b, proj_b = embed(6, ORDER[3:])
    attended, probs, part_own, part_other = pl.pallas_call(
        attend_kernel,
        in_specs=[VMEM] * 4,
        out_specs=[VMEM] * 4,
        out_shape=[
            shape((256, 1024), bf16),
            shape((4, 16, 128), f32),
            shape((64, 512), f32),
            shape((64, 512), f32),
        ],
        compiler_params=params(24),
    )(proj_a, proj_b, mix_t, rest)

    clip_part = part_own + shift(part_other, "core", 1)
    heard = {0: clip_part, **{o: shift(clip_part, "frame", o) for o in (1, 3, 2)}}
    error_own = jnp.concatenate(
        [
            sum(
                heard[o][:, SPOT[(r - o) % 4] * 128 : SPOT[(r - o) % 4] * 128 + 128]
                for o in range(4)
            )
            for r in ORDER
        ],
        axis=1,
    )
    frame_loss = jnp.mean(error_own[:, :128] * error_own[:, :128]).reshape(1, 1)
    error_other = shift(error_own, "core", 1)

    *first, delta, own_factor = pl.pallas_call(
        backward_kernel,
        in_specs=[SMEM] + [VMEM] * 9,
        out_specs=[VMEM] * 8,
        out_shape=[shape((400, 512), bf16)] * 6
        + [shape((768, 1024), bf16), shape((2, 64, 128), bf16)],
        scratch_shapes=[pltpu.VMEM((64, 1024), f32), pltpu.VMEM((256, 1024), f32)],
        compiler_params=params(40),
    )(square, error_own, error_other, proj_a, proj_b, normed_a, normed_b, probs, attended, mix)
    axes = (("x", "y"), ("y", "x"))
    moved = [[shift(first[h * 3 + k], axes[h][0], o) for k, o in enumerate((1, 3, 2))] for h in range(2)]
    kept = pl.pallas_call(
        keep_kernel,
        in_specs=[SMEM] + [VMEM] * 4,
        out_specs=[VMEM] * 2,
        out_shape=[shape((400, 512), bf16)] * 2,
        compiler_params=params(32),
        cost_estimate=cost(2 * 2 * 384 * 1024 * 512, 8 << 20),
    )(square, delta, normed_a, normed_b, own_factor)

    owned, factor = [], []
    second = [
        pl.pallas_call(
            add_first_kernel,
            in_specs=[SMEM] + [VMEM] * 4,
            out_specs=[VMEM] * 4,
            out_shape=[shape((448, 128), bf16)] * 4,
            scratch_shapes=[pltpu.VMEM((400, 512), bf16)],
        )(jnp.stack([(y, x)[h]]), kept[h], *moved[h])
        for h in range(2)
    ]
    moved = [[shift(second[h][o], axes[h][1], o) for o in (1, 3, 2)] for h in range(2)]
    for h in range(2):
        o, f = pl.pallas_call(
            add_second_kernel,
            in_specs=[VMEM] * 4,
            out_specs=[VMEM] * 2,
            out_shape=[shape((3, 128, 128), bf16), shape((128, 64), bf16)],
        )(second[h][0], *moved[h])
        owned.append(o)
        factor.append(f)
    back = [{o: shift(owned[h], axes[h][1], o) for o in (1, 3, 2)} for h in range(2)]
    line = [jnp.stack([owned[h], back[h][1], back[h][2], back[h][3]]) for h in range(2)]
    wide = [{0: line[h], **{o: shift(line[h], axes[h][0], o) for o in (1, 3, 2)}} for h in range(2)]
    theirs = [{o: shift(wide[h][o], "core", 1) for o in (0, 1, 3, 2)} for h in range(2)]

    factor = jnp.concatenate(factor)
    factor_theirs = shift(factor, "core", 1)
    factors = jnp.concatenate(
        [jnp.where(core == 0, factor, factor_theirs), jnp.where(core == 0, factor_theirs, factor)]
    )
    grad_out = dot(factors, head_t)

    def pieces(chosen):
        return [side[h][o] for o in chosen for side in (wide, theirs) for h in range(2)]

    grad_qkv = assemble(square, pieces((0, 1, 3)), (0, 1, 3))
    grad_qkv = assemble(square, pieces((2,)), (2,), grad_qkv)
    return frame_loss, grad_qkv, grad_out


def solution(mesh):
    fine = Mesh(mesh.devices.reshape(4, 4, 2, 4), ("y", "x", "core", "frame"))
    store = ("y", "x", "core")
    in_specs = (
        P((*store, "frame"), None),
        P((*store, "frame"), None),
        P((*store, "frame")),
        P(store),
        P(),
        P(),
        P(None, None, "frame"),
        P("frame", None),
        P(),
    )
    out_specs = (P(store, "frame"), P(None, None, "frame"), P("frame", None))
    return jax.shard_map(shards, mesh=fine, in_specs=in_specs, out_specs=out_specs, check_vma=False)
```

time: 342 us -> 197 us (0.58)
  waiting for transfers between devices: 232 us -> 40.3 us
  starting transfers between devices: 13.1 us -> 72.2 us
  Pallas kernels: 0 us -> 49.8 us
  matrix products: 37.3 us -> 2.7 us
  other arithmetic: 21.5 us -> 3.41 us
  between operations: 16.6 us -> 3.44 us
    psum x1 -> x0, waiting for transfers between devices: 120 us -> none  [shards(): lax.psum(grad_stack.astype(jnp.bfloat16), 'store').astype(jnp.float32)]
    ppermute x0 -> x46, starting transfers between devices: none -> 63.7 us  [shift(): lax.ppermute(value, axis, [(i, (i + offset) % size) for i in range(size)])]
    all_gather x2 -> x0, waiting for transfers between devices: 54.5 us -> none  [the longest x1 30.7 us: shards(): upstream_rows = lax.all_gather(upstream, 'frame', axis=0, tiled=True)]
    pallas_call x0 -> x14, Pallas kernels: none -> 49.8 us  [the longest x2 11.8 us: assemble(): pl.pallas_call(functools.partial(assemble_kernel, chosen, len(given)), in...]
    reduce_scatter x1 -> x0, waiting for transfers between devices: 46.9 us -> none  [shards(): lax.psum_scatter(jnp.dot(att_rows, w_out_attn, preferred_element_type=f32...]
    ppermute x0 -> x46, waiting for transfers between devices: none -> 40.3 us  [shift(): lax.ppermute(value, axis, [(i, (i + offset) % size) for i in range(size)])]
    dot_general x15 -> x1, matrix products: 33.2 us -> 2.7 us  [dot(): lax.dot_general(a, b, dims, preferred_element_type=f32, precision=precision)]
    unnamed x34 -> x67, local copies, waits for them, and re-layouts: 2.79 us -> 21.5 us
  transfers between devices with their start and end apart: 6 -> 47, of which waited for: 6 -> 12; matrix products, arithmetic and copies ran while one was open for 3% -> 4% of each run, Pallas kernels for 0% -> 16%
where the time goes in v1:
time: 197 us; the launch traced here: 195 us
  starting transfers between devices  72.2 us (37%)
  Pallas kernels  49.8 us (25%)
  waiting for transfers between devices  40.3 us (20%)
  local copies, waits for them, and re-layouts  23.6 us (12%)
  between operations  3.44 us (2%)
  other arithmetic  3.41 us (2%)
  matrix products  2.7 us (1%)
    ppermute x46, starting transfers between devices, shift(): lax.ppermute(value, axis, [(i, (i + offset) % size) for i in range(size)])  63.7 us
    ppermute x46, waiting for transfers between devices, shift(): lax.ppermute(value, axis, [(i, (i + offset) % size) for i in range(size)])  40.3 us
    unnamed x67, local copies, waits for them, and re-layouts  21.5 us
    pallas_call x2, Pallas kernels, assemble(): pl.pallas_call(functools.partial(assemble_kernel, chosen, len(given)), in...  11.8 us
    pallas_call x2, Pallas kernels, embed(): pl.pallas_call(functools.partial(embed_kernel, first, count), in_specs=[S...  9.46 us
    all_to_all x1, starting transfers between devices, shards(): lax.all_to_all(sent.reshape(128, 16, 128), ('frame', 'y', 'x', 'core'), 0...  8.49 us
    pallas_call x1, Pallas kernels, shards(): pl.pallas_call(backward_kernel, in_specs=[SMEM] + [VMEM] * 9, out_specs=[...  6.71 us
    pallas_call x1, Pallas kernels, shards(): pl.pallas_call(fetch_kernel, in_specs=[SMEM, VMEM], out_specs=VMEM, out_s...  5.22 us
  transfers between devices with their start and end apart: 47, of which 12 were waited for; matrix products, arithmetic and copies ran while one was open for 4% of the time, Pallas kernels for 16%

profile of v1, /device:TPU:1, one launch (start us, length us, event | category | flops | bytes accessed | tf_op | source)
XLA Modules:
  0.0 195.4 jit_solution(13014917457728425803)
XLA Ops:
  0.6 4.5 %collective-permute-start.6 = (bf16[128,2048]{1,0:T(8,128)(2,1)}, bf16[128,2048]{1,0:T(8,128)(2,1)}, u32[]{:S(2)}, u32[]{:S(2)}) collective-permute-start(bf16[128,2048]{1,0:T(8,128)(2,1)} %refs_0_.1), channel_id=1, source_target_pairs={{0,2},{1,3},{2,0},{3,1},{4,6},{5,7},{6,4},{7,5},{8,10},{9,11},{10,... | collective-permute-start | bytes 1572872 | tf_op jit(solution)/shard_map/ppermute | solution.py:41
  5.9 1.9 collective-permute-start.4
  7.8 1.4 copy.13.dest_col
  9.2 1.9 shard_map.112
  11.1 8.5 %all-to-all-start = ((bf16[128,16,128]{2,1,0:T(8,128)(2,1)}), bf16[128,16,128]{2,1,0:T(8,128)(2,1)}, u32[]{:S(2)}, u32[]{:S(2)}) async-start(bf16[128,16,128]{2,1,0:T(8,128)(2,1)} %bitcast.28), calls=%async_computation | async-start | bytes 1048576 | tf_op jit(solution)/shard_map/all_to_all | solution.py:303
  21.0 13.5 %collective-permute-done.2.refs_2_ = bf16[128,2048]{1,0:T(8,128)(2,1)} collective-permute-done((bf16[128,2048]{1,0:T(8,128)(2,1)}, bf16[128,2048]{1,0:T(8,128)(2,1)}, u32[]{:S(2)}, u32[]{:S(2)}) %collective-permute-start.2) | collective-permute-done | bytes 524320 | tf_op jit(solution)/shard_map/ppermute | solution.py:41
  37.6 2.8 %copy-done = bf16[3,2048,512]{2,1,0:T(8,128)(2,1)S(1)} copy-done((bf16[3,2048,512]{2,1,0:T(8,128)(2,1)S(1)}, bf16[3,2048,512]{2,1,0:T(8,128)(2,1)}, u32[]{:S(2)}) %copy-start) | copy-done | bytes 6291480
  41.3 1.6 copy-done.9
  42.9 2.7 %shard_map.114 = (bf16[2,3,128,2048]{3,2,1,0:T(8,128)(2,1)S(1)}, f32[256,64]{1,0:T(8,128)S(1)}, f32[64,256]{1,0:T(8,128)S(1)}) custom-call(s32[2]{0:T(128)S(1)} %pad_add_fusion.place, bf16[3,2048,512]{2,1,0:T(8,128)(2,1)S(1)} %copy-done, bf16[512,2048]{1,0:T(8,128)(2,1)S(1)} %copy-done.9, bf16[64,2048]{1,0:T(8,128)(2,1)S(1)} %bitcast.23), custom_call_target="tpu_custom_call" | custom-call | flops 134217728 | bytes 8388608 | tf_op jit(solution)/shard_map/pallas_call | solution.py:310
  47.0 5.2 %shard_map.113.refs_6_.refs_2_ = bf16[8,128,128]{2,1,0:T(8,128)(2,1)S(1)} custom-call(s32[2]{0:T(128)S(1)} %pad_add_fusion.place, bf16[4,512,128]{2,1,0:T(8,128)(2,1)} %bitcast.5.arrived), custom_call_target="tpu_custom_call" | custom-call | flops 600000000 | bytes 1048576 | tf_op jit(solution)/shard_map/pallas_call | solution.py:332
  53.2 2.8 %shard_map.116 = (bf16[256,2048]{1,0:T(8,128)(2,1)S(1)}, bf16[768,256]{1,0:T(8,128)(2,1)S(1)}) custom-call(f32[2]{0:T(128)S(1)} %pad_maximum_fusion.3.moments, bf16[128,2048]{1,0:T(8,128)(2,1)} %collective-permute-done.6.refs_0_, bf16[128,2048]{1,0:T(8,128)(2,1)} %collective-permute-done.7.refs_1_, bf16[8,128,128]{2,1,0:T(8,128)(2,1)S(1)} %shard_map.113.refs_6_.refs_2_, ...), custom_call_target="tpu_custom_call" | custom-call | flops 805306368 | bytes 5242880 | tf_op jit(solution)/shard_map/pallas_call | solution.py:347
  57.1 2.0 %copy-done.6 = bf16[2,3,128,2048]{3,2,1,0:T(8,128)(2,1)S(1)} copy-done((bf16[2,3,128,2048]{3,2,1,0:T(8,128)(2,1)S(1)}, bf16[2,3,128,2048]{3,2,1,0:T(8,128)(2,1)}, u32[]{:S(2)}) %copy-start.6) | copy-done | bytes 3145752
  59.1 6.6 %shard_map.115 = (bf16[768,2048]{1,0:T(8,128)(2,1)S(1)}, bf16[768,768]{1,0:T(8,128)(2,1)S(1)}, f32[64,128]{1,0:T(8,128)S(1)}) custom-call(f32[2]{0:T(128)S(1)} %pad_maximum_fusion.3.moments, bf16[128,2048]{1,0:T(8,128)(2,1)S(1)} %copy-done.23, bf16[128,2048]{1,0:T(8,128)(2,1)} %collective-permute-done.1.refs_1_, ...), custom_call_target="tpu_custom_call" | custom-call | flops 2415919104 | bytes 9437184 | tf_op jit(solution)/shard_map/pallas_call | solution.py:347
  65.7 1.7 shard_map.117
  70.0 2.4 %collective-permute-start.11 = (f32[64,512]{1,0:T(8,128)S(1)}, f32[64,512]{1,0:T(8,128)S(1)}, u32[]{:S(2)}, u32[]{:S(2)}) collective-permute-start(f32[64,512]{1,0:T(8,128)S(1)} %add.43), channel_id=1, source_target_pairs={{0,3},{1,0},{2,1},{3,2},{4,7},{5,4},{6,5},{7,6},{8,11},{9,8},{10,9... | collective-permute-start | bytes 393224 | tf_op jit(solution)/shard_map/ppermute | solution.py:41
  73.1 2.5 %collective-permute-done.11 = f32[64,512]{1,0:T(8,128)S(1)} collective-permute-done((f32[64,512]{1,0:T(8,128)S(1)}, f32[64,512]{1,0:T(8,128)S(1)}, u32[]{:S(2)}, u32[]{:S(2)}) %collective-permute-start.11) | collective-permute-done | bytes 131104 | tf_op jit(solution)/shard_map/ppermute | solution.py:41
  75.6 2.7 %collective-permute-done.10 = f32[64,512]{1,0:T(8,128)S(1)} collective-permute-done((f32[64,512]{1,0:T(8,128)S(1)}, f32[64,512]{1,0:T(8,128)S(1)}, u32[]{:S(2)}, u32[]{:S(2)}) %collective-permute-start.10) | collective-permute-done | bytes 131104 | tf_op jit(solution)/shard_map/ppermute | solution.py:41
  78.3 3.8 %collective-permute-done.9 = f32[64,512]{1,0:T(8,128)S(1)} collective-permute-done((f32[64,512]{1,0:T(8,128)S(1)}, f32[64,512]{1,0:T(8,128)S(1)}, u32[]{:S(2)}, u32[]{:S(2)}) %collective-permute-start.9) | collective-permute-done | bytes 131104 | tf_op jit(solution)/shard_map/ppermute | solution.py:41
  84.5 1.3 copy-done.2
  90.7 6.7 %shard_map.118 = (bf16[400,512]{1,0:T(8,128)(2,1)S(1)}, bf16[400,512]{1,0:T(8,128)(2,1)S(1)}, bf16[400,512]{1,0:T(8,128)(2,1)S(1)}, bf16[400,512]{1,0:T(8,128)(2...) custom-call(s32[3]{0:T(128)S(1)} %pad_add_fusion.1.place, ...), custom_call_target="tpu_custom_call" | custom-call | tf_op jit(solution)/shard_map/pallas_call | solution.py:386
  98.6 1.4 collective-permute-start.14
  100.0 1.5 collective-permute-start.15
  101.6 1.3 collective-permute-start.23
  102.9 1.5 collective-permute-start.24
  104.4 5.0 %collective-permute-done.13.refs_1_ = bf16[400,512]{1,0:T(8,128)(2,1)S(1)} collective-permute-done((bf16[400,512]{1,0:T(8,128)(2,1)S(1)}, bf16[400,512]{1,0:T(8,128)(2,1)S(1)}, u32[]{:S(2)}, u32[]{:S(2)}) %collective-permute-start.13) | collective-permute-done | bytes 409632 | tf_op jit(solution)/shard_map/ppermute | solution.py:41
  109.4 2.8 %collective-permute-start.25 = (bf16[400,512]{1,0:T(8,128)(2,1)}, bf16[400,512]{1,0:T(8,128)(2,1)}, u32[]{:S(2)}, u32[]{:S(2)}) collective-permute-start(bf16[400,512]{1,0:T(8,128)(2,1)} %get-tuple-element.63), channel_id=1, source_target_pairs={{0,64},{32,96},{64,0},{96,32},{1,65},{33,97},{65,1},{97,33},{2,66}... | collective-permute-start | bytes 1228808 | tf_op jit(solution)/shard_map/ppermute | solution.py:41
  112.2 1.5 shard_map.119
  115.2 3.9 %collective-permute-done.15.refs_3_ = bf16[400,512]{1,0:T(8,128)(2,1)S(1)} collective-permute-done((bf16[400,512]{1,0:T(8,128)(2,1)S(1)}, bf16[400,512]{1,0:T(8,128)(2,1)S(1)}, u32[]{:S(2)}, u32[]{:S(2)}) %collective-permute-start.15) | collective-permute-done | bytes 409632 | tf_op jit(solution)/shard_map/ppermute | solution.py:41
  119.9 2.6 %shard_map.120 = (bf16[448,128]{1,0:T(8,128)(2,1)}, bf16[448,128]{1,0:T(8,128)(2,1)}, bf16[448,128]{1,0:T(8,128)(2,1)}, bf16[448,128]{1,0:T(8,128)(2,1)}) custom-call(s32[1]{0:T(128)} %bitcast.11.place, bf16[400,512]{1,0:T(8,128)(2,1)} %copy-done.15, bf16[400,512]{1,0:T(8,128)(2,1)} %copy-done.24, bf16[400,512]{1,0:T(8,128)(2,1)} %copy-done.25, ...), custom_call_target="tpu_custom_call" | custom-call | tf_op jit(solution)/shard_map/pallas_call | solution.py:408
  123.7 1.6 collective-permute-start.17
  125.3 1.5 collective-permute-start.18
  126.8 2.6 %shard_map.122 = (bf16[448,128]{1,0:T(8,128)(2,1)}, bf16[448,128]{1,0:T(8,128)(2,1)}, bf16[448,128]{1,0:T(8,128)(2,1)}, bf16[448,128]{1,0:T(8,128)(2,1)}) custom-call(s32[1]{0:T(128)} %bitcast.10.place, bf16[400,512]{1,0:T(8,128)(2,1)} %copy-done.14, bf16[400,512]{1,0:T(8,128)(2,1)} %collective-permute-done.23.refs_1_, ...), custom_call_target="tpu_custom_call" | custom-call | tf_op jit(solution)/shard_map/pallas_call | solution.py:408
  130.0 2.0 %collective-permute-start.27 = (bf16[448,128]{1,0:T(8,128)(2,1)}, bf16[448,128]{1,0:T(8,128)(2,1)S(1)}, u32[]{:S(2)}, u32[]{:S(2)}) collective-permute-start(bf16[448,128]{1,0:T(8,128)(2,1)} %get-tuple-element.66), channel_id=1, source_target_pairs={{0,24},{8,0},{16,8},{24,16},{1,25},{9,1},{17,9},{25,17},{2,26},{10... | collective-permute-start | bytes 344072 | tf_op jit(solution)/shard_map/ppermute | solution.py:41
  132.7 1.8 shard_map.121
  134.6 1.4 collective-permute-start.21
  136.9 1.3 collective-permute-done.28.refs_3_
  138.9 1.9 shard_map.123
  144.2 2.6 %collective-permute-start.22 = (bf16[4,3,128,128]{3,2,1,0:T(8,128)(2,1)S(1)}, bf16[4,3,128,128]{3,2,1,0:T(8,128)(2,1)S(1)}, u32[]{:S(2)}, u32[]{:S(2)}) collective-permute-start(bf16[4,3,128,128]{3,2,1,0:T(8,128)(2,1)S(1)} %pad_maximum_fusion.refs_0_), channel_id=1, source_target_pairs={{0,16},{8,24},{16,0},{24,8},{1,17},{9,25},{17,1},{25,9},{2,18},{10... | collective-permute-start | bytes 1179656 | tf_op jit(solution)/shard_map/ppermute | solution.py:41
  148.3 2.9 %collective-permute-start.32 = (bf16[4,3,128,128]{3,2,1,0:T(8,128)(2,1)S(1)}, bf16[4,3,128,128]{3,2,1,0:T(8,128)(2,1)S(1)}, u32[]{:S(2)}, u32[]{:S(2)}) collective-permute-start(bf16[4,3,128,128]{3,2,1,0:T(8,128)(2,1)S(1)} %pad_maximum_fusion.1.refs_1_), channel_id=1, source_target_pairs={{0,64},{32,96},{64,0},{96,32},{1,65},{33,97},{65,1},{97,33},{2,66}... | collective-permute-start | bytes 1179656 | tf_op jit(solution)/shard_map/ppermute | solution.py:41
  151.2 7.8 %collective-permute-start.35 = (bf16[4,3,128,128]{3,2,1,0:T(8,128)(2,1)S(1)}, bf16[4,3,128,128]{3,2,1,0:T(8,128)(2,1)S(1)}, u32[]{:S(2)}, u32[]{:S(2)}) collective-permute-start(bf16[4,3,128,128]{3,2,1,0:T(8,128)(2,1)S(1)} %pad_maximum_fusion.refs_0_), channel_id=1, source_target_pairs={{0,4},{4,0},{1,5},{5,1},{2,6},{6,2},{3,7},{7,3},{8,12},{12,8},{9,1... | collective-permute-start | bytes 1179656 | tf_op jit(solution)/shard_map/ppermute | solution.py:41
  162.6 5.5 %collective-permute-start.41 = (bf16[4,3,128,128]{3,2,1,0:T(8,128)(2,1)S(1)}, bf16[4,3,128,128]{3,2,1,0:T(8,128)(2,1)}, u32[]{:S(2)}, u32[]{:S(2)}) collective-permute-start(bf16[4,3,128,128]{3,2,1,0:T(8,128)(2,1)S(1)} %pad_maximum_fusion.refs_0_), channel_id=1, source_target_pairs={{0,24},{8,0},{16,8},{24,16},{1,25},{9,1},{17,9},{25,17},{2,26},{10... | collective-permute-start | bytes 1179656 | tf_op jit(solution)/shard_map/ppermute | solution.py:41
  168.1 2.3 %collective-permute-start.42 = (bf16[4,3,128,128]{3,2,1,0:T(8,128)(2,1)S(1)}, bf16[4,3,128,128]{3,2,1,0:T(8,128)(2,1)}, u32[]{:S(2)}, u32[]{:S(2)}) collective-permute-start(bf16[4,3,128,128]{3,2,1,0:T(8,128)(2,1)S(1)} %pad_maximum_fusion.1.refs_1_), channel_id=1, source_target_pairs={{0,96},{32,0},{64,32},{96,64},{1,97},{33,1},{65,33},{97,65},{2,98}... | collective-permute-start | bytes 1179656 | tf_op jit(solution)/shard_map/ppermute | solution.py:41
  170.3 3.9 %collective-permute-done.37.refs_4_ = bf16[4,3,128,128]{3,2,1,0:T(8,128)(2,1)S(1)} collective-permute-done((bf16[4,3,128,128]{3,2,1,0:T(8,128)(2,1)S(1)}, bf16[4,3,128,128]{3,2,1,0:T(8,128)(2,1)S(1)}, u32[]{:S(2)}, u32[]{:S(2)}) %collective-permute-start.37) | collective-permute-done | bytes 393248 | tf_op jit(solution)/shard_map/ppermute | solution.py:41
  176.0 1.4 collective-permute-start.40
  177.4 2.3 %collective-permute-start.43 = (bf16[4,3,128,128]{3,2,1,0:T(8,128)(2,1)}, bf16[4,3,128,128]{3,2,1,0:T(8,128)(2,1)S(1)}, u32[]{:S(2)}, u32[]{:S(2)}) collective-permute-start(bf16[4,3,128,128]{3,2,1,0:T(8,128)(2,1)} %collective-permute-done.41.refs_8_), channel_id=1, source_target_pairs={{0,4},{4,0},{1,5},{5,1},{2,6},{6,2},{3,7},{7,3},{8,12},{12,8},{9,1... | collective-permute-start | bytes 1179656 | tf_op jit(solution)/shard_map/ppermute | solution.py:41
  179.7 2.7 %fusion = f32[512,2048]{1,0:T(8,128)} fusion(bf16[2048,64]{0,1:T(8,128)(2,1)S(1)} %copy-done.8, bf16[256,64]{1,0:T(8,128)(2,1)S(1)} %get-tuple-element.79, bf16[256,64]{1,0:T(8,128)(2,1)S(1)} %get-tuple-element.78), kind=kOutput, calls=%fused_computation.3 | convolution fusion | flops 134348800 | bytes 4521984 | tf_op jit(solution)/shard_map/dot_general | solution.py:36
  182.5 8.3 %shard_map.124.refs_4_ = f32[3,2048,512]{2,1,0:T(8,128)} custom-call(s32[3]{0:T(128)S(1)} %pad_add_fusion.1.place, bf16[4,3,128,128]{3,2,1,0:T(8,128)(2,1)S(1)} %pad_maximum_fusion.refs_0_, bf16[4,3,128,128]{3,2,1,0:T(8,128)(2,1)S(1)} %pad_maximum_fusion.1.refs_1_, bf16[4,3,128,128]{3,2,1,0:T(8,128)(2,1)S(1)} %collective-permute-done.35.refs_2_, ...), custom_call_target="tpu_custom_call" | custom-call | bytes 14155776 | tf_op jit(solution)/shard_map/pallas_call | solution.py:272
  190.8 3.5 %shard_map.125 = f32[3,2048,512]{2,1,0:T(8,128)} custom-call(s32[3]{0:T(128)S(1)} %pad_add_fusion.1.place, bf16[4,3,128,128]{3,2,1,0:T(8,128)(2,1)S(1)} %collective-permute-done.22.refs_0_, bf16[4,3,128,128]{3,2,1,0:T(8,128)(2,1)S(1)} %collective-permute-done.32.refs_1_, ...), custom_call_target="tpu_custom_call", output_to_operand_aliasing={{}: (5, {})} | custom-call | bytes 4718592 | tf_op jit(solution)/shard_map/pallas_call | solution.py:272
  (139 shorter events, 36.7 us)
Async XLA Ops:
  0.6 19.0 %collective-permute-start.6 = (bf16[128,2048]{1,0:T(8,128)(2,1)}, bf16[128,2048]{1,0:T(8,128)(2,1)}, u32[]{:S(2)}, u32[]{:S(2)}) collective-permute-start(bf16[128,2048]{1,0:T(8,128)(2,1)} %refs_0_.1), channel_id=1, source_target_pairs={{0,2},{1,3},{2,0},{3,1},{4,6},{5,7},{6,4},{7,5},{8,10},{9,11},{10,... | collective-permute-start | bytes 1572872 | tf_op jit(solution)/shard_map/ppermute | solution.py:41
  5.1 29.3 %collective-permute-start.2 = (bf16[128,2048]{1,0:T(8,128)(2,1)}, bf16[128,2048]{1,0:T(8,128)(2,1)}, u32[]{:S(2)}, u32[]{:S(2)}) collective-permute-start(bf16[128,2048]{1,0:T(8,128)(2,1)} %refs_0_.1), channel_id=1, source_target_pairs={{0,1},{1,2},{2,3},{3,0},{4,5},{5,6},{6,7},{7,4},{8,9},{9,10},{10,1... | collective-permute-start | bytes 1572872 | tf_op jit(solution)/shard_map/ppermute | solution.py:41
  5.9 29.1 %collective-permute-start.4 = (bf16[128,2048]{1,0:T(8,128)(2,1)}, bf16[128,2048]{1,0:T(8,128)(2,1)}, u32[]{:S(2)}, u32[]{:S(2)}) collective-permute-start(bf16[128,2048]{1,0:T(8,128)(2,1)} %refs_0_.1), channel_id=1, source_target_pairs={{0,3},{1,0},{2,1},{3,2},{4,7},{5,4},{6,5},{7,6},{8,11},{9,8},{10,9... | collective-permute-start | bytes 1572872 | tf_op jit(solution)/shard_map/ppermute | solution.py:41
  11.1 35.9 %all-to-all-start = ((bf16[128,16,128]{2,1,0:T(8,128)(2,1)}), bf16[128,16,128]{2,1,0:T(8,128)(2,1)}, u32[]{:S(2)}, u32[]{:S(2)}) async-start(bf16[128,16,128]{2,1,0:T(8,128)(2,1)} %bitcast.28), calls=%async_computation | async-start | bytes 1048576 | tf_op jit(solution)/shard_map/all_to_all | solution.py:303
  19.6 32.6 %collective-permute-start.7 = (bf16[128,2048]{1,0:T(8,128)(2,1)}, bf16[128,2048]{1,0:T(8,128)(2,1)}, u32[]{:S(2)}, u32[]{:S(2)}) collective-permute-start(bf16[128,2048]{1,0:T(8,128)(2,1)} %collective-permute-done.6.refs_0_), channel_id=1, source_target_pairs={{0,4},{4,0},{1,5},{5,1},{2,6},{6,2},{3,7},{7,3},{8,12},{12,8},{9,1... | collective-permute-start | bytes 1572872 | tf_op jit(solution)/shard_map/ppermute | solution.py:41
  20.9 36.2 %collective-permute-start.1 = (bf16[128,2048]{1,0:T(8,128)(2,1)}, bf16[128,2048]{1,0:T(8,128)(2,1)}, u32[]{:S(2)}, u32[]{:S(2)}) collective-permute-start(bf16[128,2048]{1,0:T(8,128)(2,1)} %refs_0_.1), channel_id=1, source_target_pairs={{0,4},{4,0},{1,5},{5,1},{2,6},{6,2},{3,7},{7,3},{8,12},{12,8},{9,1... | collective-permute-start | bytes 1572872 | tf_op jit(solution)/shard_map/ppermute | solution.py:41
  34.4 22.6 %collective-permute-start.3 = (bf16[128,2048]{1,0:T(8,128)(2,1)}, bf16[128,2048]{1,0:T(8,128)(2,1)}, u32[]{:S(2)}, u32[]{:S(2)}) collective-permute-start(bf16[128,2048]{1,0:T(8,128)(2,1)} %collective-permute-done.2.refs_2_), channel_id=1, source_target_pairs={{0,4},{4,0},{1,5},{5,1},{2,6},{6,2},{3,7},{7,3},{8,12},{12,8},{9,1... | collective-permute-start | bytes 1572872 | tf_op jit(solution)/shard_map/ppermute | solution.py:41
  35.0 22.0 %collective-permute-start.5 = (bf16[128,2048]{1,0:T(8,128)(2,1)}, bf16[128,2048]{1,0:T(8,128)(2,1)}, u32[]{:S(2)}, u32[]{:S(2)}) collective-permute-start(bf16[128,2048]{1,0:T(8,128)(2,1)} %collective-permute-done.4.refs_4_), channel_id=1, source_target_pairs={{0,4},{4,0},{1,5},{5,1},{2,6},{6,2},{3,7},{7,3},{8,12},{12,8},{9,1... | collective-permute-start | bytes 1572872 | tf_op jit(solution)/shard_map/ppermute | solution.py:41
  36.4 9.8 %collective-permute-start = (f32[1]{0:T(128)}, f32[1]{0:T(128)}, u32[]{:S(2)}, u32[]{:S(2)}) collective-permute-start(f32[1]{0:T(128)} %div.6), channel_id=1, source_target_pairs={{0,4},{4,0},{1,5},{5,1},{2,6},{6,2},{3,7},{7,3},{8,12},{12,8},{9,1... | collective-permute-start | bytes 20 | tf_op jit(solution)/shard_map/ppermute | solution.py:41
  68.5 14.3 %copy-start.20 = (f32[4,16,128]{2,1,0:T(8,128)}, f32[4,16,128]{2,1,0:T(8,128)S(1)}, u32[]{:S(2)}) copy-start(f32[4,16,128]{2,1,0:T(8,128)S(1)} %get-tuple-element.46.probs) | copy-start | bytes 98308
  68.5 1.5 collective-permute-start.8
  70.0 5.6 %collective-permute-start.11 = (f32[64,512]{1,0:T(8,128)S(1)}, f32[64,512]{1,0:T(8,128)S(1)}, u32[]{:S(2)}, u32[]{:S(2)}) collective-permute-start(f32[64,512]{1,0:T(8,128)S(1)} %add.43), channel_id=1, source_target_pairs={{0,3},{1,0},{2,1},{3,2},{4,7},{5,4},{6,5},{7,6},{8,11},{9,8},{10,9... | collective-permute-start | bytes 393224 | tf_op jit(solution)/shard_map/ppermute | solution.py:41
  72.4 5.9 %collective-permute-start.10 = (f32[64,512]{1,0:T(8,128)S(1)}, f32[64,512]{1,0:T(8,128)S(1)}, u32[]{:S(2)}, u32[]{:S(2)}) collective-permute-start(f32[64,512]{1,0:T(8,128)S(1)} %add.43), channel_id=1, source_target_pairs={{0,2},{1,3},{2,0},{3,1},{4,6},{5,7},{6,4},{7,5},{8,10},{9,11},{10,... | collective-permute-start | bytes 393224 | tf_op jit(solution)/shard_map/ppermute | solution.py:41
  73.0 9.2 %collective-permute-start.9 = (f32[64,512]{1,0:T(8,128)S(1)}, f32[64,512]{1,0:T(8,128)S(1)}, u32[]{:S(2)}, u32[]{:S(2)}) collective-permute-start(f32[64,512]{1,0:T(8,128)S(1)} %add.43), channel_id=1, source_target_pairs={{0,1},{1,2},{2,3},{3,0},{4,5},{5,6},{6,7},{7,4},{8,9},{9,10},{10,1... | collective-permute-start | bytes 393224 | tf_op jit(solution)/shard_map/ppermute | solution.py:41
  82.8 1.7 collective-permute-start.12
  97.4 12.0 %collective-permute-start.13 = (bf16[400,512]{1,0:T(8,128)(2,1)S(1)}, bf16[400,512]{1,0:T(8,128)(2,1)S(1)}, u32[]{:S(2)}, u32[]{:S(2)}) collective-permute-start(bf16[400,512]{1,0:T(8,128)(2,1)S(1)} %get-tuple-element.52), channel_id=1, source_target_pairs={{0,8},{8,16},{16,24},{24,0},{1,9},{9,17},{17,25},{25,1},{2,10},{10... | collective-permute-start | bytes 1228808 | tf_op jit(solution)/shard_map/ppermute | solution.py:41
  98.6 16.6 %collective-permute-start.14 = (bf16[400,512]{1,0:T(8,128)(2,1)S(1)}, bf16[400,512]{1,0:T(8,128)(2,1)S(1)}, u32[]{:S(2)}, u32[]{:S(2)}) collective-permute-start(bf16[400,512]{1,0:T(8,128)(2,1)S(1)} %get-tuple-element.53), channel_id=1, source_target_pairs={{0,24},{8,0},{16,8},{24,16},{1,25},{9,1},{17,9},{25,17},{2,26},{10... | collective-permute-start | bytes 1228808 | tf_op jit(solution)/shard_map/ppermute | solution.py:41
  100.0 19.1 %collective-permute-start.15 = (bf16[400,512]{1,0:T(8,128)(2,1)S(1)}, bf16[400,512]{1,0:T(8,128)(2,1)S(1)}, u32[]{:S(2)}, u32[]{:S(2)}) collective-permute-start(bf16[400,512]{1,0:T(8,128)(2,1)S(1)} %get-tuple-element.54), channel_id=1, source_target_pairs={{0,16},{8,24},{16,0},{24,8},{1,17},{9,25},{17,1},{25,9},{2,18},{10... | collective-permute-start | bytes 1228808 | tf_op jit(solution)/shard_map/ppermute | solution.py:41
  101.6 23.7 %collective-permute-start.23 = (bf16[400,512]{1,0:T(8,128)(2,1)}, bf16[400,512]{1,0:T(8,128)(2,1)}, u32[]{:S(2)}, u32[]{:S(2)}) collective-permute-start(bf16[400,512]{1,0:T(8,128)(2,1)} %get-tuple-element.61), channel_id=1, source_target_pairs={{0,32},{32,64},{64,96},{96,0},{1,33},{33,65},{65,97},{97,1},{2,34}... | collective-permute-start | bytes 1228808 | tf_op jit(solution)/shard_map/ppermute | solution.py:41
  102.9 23.9 %collective-permute-start.24 = (bf16[400,512]{1,0:T(8,128)(2,1)}, bf16[400,512]{1,0:T(8,128)(2,1)}, u32[]{:S(2)}, u32[]{:S(2)}) collective-permute-start(bf16[400,512]{1,0:T(8,128)(2,1)} %get-tuple-element.62), channel_id=1, source_target_pairs={{0,96},{32,0},{64,32},{96,64},{1,97},{33,1},{65,33},{97,65},{2,98}... | collective-permute-start | bytes 1228808 | tf_op jit(solution)/shard_map/ppermute | solution.py:41
  109.4 17.4 %collective-permute-start.25 = (bf16[400,512]{1,0:T(8,128)(2,1)}, bf16[400,512]{1,0:T(8,128)(2,1)}, u32[]{:S(2)}, u32[]{:S(2)}) collective-permute-start(bf16[400,512]{1,0:T(8,128)(2,1)} %get-tuple-element.63), channel_id=1, source_target_pairs={{0,64},{32,96},{64,0},{96,32},{1,65},{33,97},{65,1},{97,33},{2,66}... | collective-permute-start | bytes 1228808 | tf_op jit(solution)/shard_map/ppermute | solution.py:41
  122.5 9.5 %collective-permute-start.16 = (bf16[448,128]{1,0:T(8,128)(2,1)}, bf16[448,128]{1,0:T(8,128)(2,1)S(1)}, u32[]{:S(2)}, u32[]{:S(2)}) collective-permute-start(bf16[448,128]{1,0:T(8,128)(2,1)} %get-tuple-element.56), channel_id=1, source_target_pairs={{0,32},{32,64},{64,96},{96,0},{1,33},{33,65},{65,97},{97,1},{2,34}... | collective-permute-start | bytes 344072 | tf_op jit(solution)/shard_map/ppermute | solution.py:41
  123.7 8.3 %collective-permute-start.17 = (bf16[448,128]{1,0:T(8,128)(2,1)}, bf16[448,128]{1,0:T(8,128)(2,1)S(1)}, u32[]{:S(2)}, u32[]{:S(2)}) collective-permute-start(bf16[448,128]{1,0:T(8,128)(2,1)} %get-tuple-element.57), channel_id=1, source_target_pairs={{0,96},{32,0},{64,32},{96,64},{1,97},{33,1},{65,33},{97,65},{2,98}... | collective-permute-start | bytes 344072 | tf_op jit(solution)/shard_map/ppermute | solution.py:41
  125.3 6.8 %collective-permute-start.18 = (bf16[448,128]{1,0:T(8,128)(2,1)}, bf16[448,128]{1,0:T(8,128)(2,1)S(1)}, u32[]{:S(2)}, u32[]{:S(2)}) collective-permute-start(bf16[448,128]{1,0:T(8,128)(2,1)} %get-tuple-element.58), channel_id=1, source_target_pairs={{0,64},{32,96},{64,0},{96,32},{1,65},{33,97},{65,1},{97,33},{2,66}... | collective-permute-start | bytes 344072 | tf_op jit(solution)/shard_map/ppermute | solution.py:41
  129.3 7.5 %collective-permute-start.26 = (bf16[448,128]{1,0:T(8,128)(2,1)}, bf16[448,128]{1,0:T(8,128)(2,1)S(1)}, u32[]{:S(2)}, u32[]{:S(2)}) collective-permute-start(bf16[448,128]{1,0:T(8,128)(2,1)} %get-tuple-element.65), channel_id=1, source_target_pairs={{0,8},{8,16},{16,24},{24,0},{1,9},{9,17},{17,25},{25,1},{2,10},{10... | collective-permute-start | bytes 344072 | tf_op jit(solution)/shard_map/ppermute | solution.py:41
  130.0 6.9 %collective-permute-start.27 = (bf16[448,128]{1,0:T(8,128)(2,1)}, bf16[448,128]{1,0:T(8,128)(2,1)S(1)}, u32[]{:S(2)}, u32[]{:S(2)}) collective-permute-start(bf16[448,128]{1,0:T(8,128)(2,1)} %get-tuple-element.66), channel_id=1, source_target_pairs={{0,24},{8,0},{16,8},{24,16},{1,25},{9,1},{17,9},{25,17},{2,26},{10... | collective-permute-start | bytes 344072 | tf_op jit(solution)/shard_map/ppermute | solution.py:41
  132.0 6.2 %collective-permute-start.28 = (bf16[448,128]{1,0:T(8,128)(2,1)}, bf16[448,128]{1,0:T(8,128)(2,1)S(1)}, u32[]{:S(2)}, u32[]{:S(2)}) collective-permute-start(bf16[448,128]{1,0:T(8,128)(2,1)} %get-tuple-element.67), channel_id=1, source_target_pairs={{0,16},{8,24},{16,0},{24,8},{1,17},{9,25},{17,1},{25,9},{2,18},{10... | collective-permute-start | bytes 344072 | tf_op jit(solution)/shard_map/ppermute | solution.py:41
  134.6 7.8 %collective-permute-start.21 = (bf16[3,128,128]{2,1,0:T(8,128)(2,1)}, bf16[3,128,128]{2,1,0:T(8,128)(2,1)S(1)}, u32[]{:S(2)}, u32[]{:S(2)}) collective-permute-start(bf16[3,128,128]{2,1,0:T(8,128)(2,1)} %get-tuple-element.59), channel_id=1, source_target_pairs={{0,96},{32,0},{64,32},{96,64},{1,97},{33,1},{65,33},{97,65},{2,98}... | collective-permute-start | bytes 294920 | tf_op jit(solution)/shard_map/ppermute | solution.py:41
  136.0 7.3 %collective-permute-start.20 = (bf16[3,128,128]{2,1,0:T(8,128)(2,1)}, bf16[3,128,128]{2,1,0:T(8,128)(2,1)S(1)}, u32[]{:S(2)}, u32[]{:S(2)}) collective-permute-start(bf16[3,128,128]{2,1,0:T(8,128)(2,1)} %get-tuple-element.59), channel_id=1, source_target_pairs={{0,64},{32,96},{64,0},{96,32},{1,65},{33,97},{65,1},{97,33},{2,66}... | collective-permute-start | bytes 294920 | tf_op jit(solution)/shard_map/ppermute | solution.py:41
  136.9 6.4 %collective-permute-start.19 = (bf16[3,128,128]{2,1,0:T(8,128)(2,1)}, bf16[3,128,128]{2,1,0:T(8,128)(2,1)S(1)}, u32[]{:S(2)}, u32[]{:S(2)}) collective-permute-start(bf16[3,128,128]{2,1,0:T(8,128)(2,1)} %get-tuple-element.59), channel_id=1, source_target_pairs={{0,32},{32,64},{64,96},{96,0},{1,33},{33,65},{65,97},{97,1},{2,34}... | collective-permute-start | bytes 294920 | tf_op jit(solution)/shard_map/ppermute | solution.py:41
  140.7 6.1 %collective-permute-start.31 = (bf16[3,128,128]{2,1,0:T(8,128)(2,1)}, bf16[3,128,128]{2,1,0:T(8,128)(2,1)S(1)}, u32[]{:S(2)}, u32[]{:S(2)}) collective-permute-start(bf16[3,128,128]{2,1,0:T(8,128)(2,1)} %get-tuple-element.68), channel_id=1, source_target_pairs={{0,24},{8,0},{16,8},{24,16},{1,25},{9,1},{17,9},{25,17},{2,26},{10... | collective-permute-start | bytes 294920 | tf_op jit(solution)/shard_map/ppermute | solution.py:41
  141.1 5.7 %collective-permute-start.30 = (bf16[3,128,128]{2,1,0:T(8,128)(2,1)}, bf16[3,128,128]{2,1,0:T(8,128)(2,1)S(1)}, u32[]{:S(2)}, u32[]{:S(2)}) collective-permute-start(bf16[3,128,128]{2,1,0:T(8,128)(2,1)} %get-tuple-element.68), channel_id=1, source_target_pairs={{0,16},{8,24},{16,0},{24,8},{1,17},{9,25},{17,1},{25,9},{2,18},{10... | collective-permute-start | bytes 294920 | tf_op jit(solution)/shard_map/ppermute | solution.py:41
  142.4 5.0 %collective-permute-start.29 = (bf16[3,128,128]{2,1,0:T(8,128)(2,1)}, bf16[3,128,128]{2,1,0:T(8,128)(2,1)S(1)}, u32[]{:S(2)}, u32[]{:S(2)}) collective-permute-start(bf16[3,128,128]{2,1,0:T(8,128)(2,1)} %get-tuple-element.68), channel_id=1, source_target_pairs={{0,8},{8,16},{16,24},{24,0},{1,9},{9,17},{17,25},{25,1},{2,10},{10... | collective-permute-start | bytes 294920 | tf_op jit(solution)/shard_map/ppermute | solution.py:41
  144.2 17.9 %collective-permute-start.22 = (bf16[4,3,128,128]{3,2,1,0:T(8,128)(2,1)S(1)}, bf16[4,3,128,128]{3,2,1,0:T(8,128)(2,1)S(1)}, u32[]{:S(2)}, u32[]{:S(2)}) collective-permute-start(bf16[4,3,128,128]{3,2,1,0:T(8,128)(2,1)S(1)} %pad_maximum_fusion.refs_0_), channel_id=1, source_target_pairs={{0,16},{8,24},{16,0},{24,8},{1,17},{9,25},{17,1},{25,9},{2,18},{10... | collective-permute-start | bytes 1179656 | tf_op jit(solution)/shard_map/ppermute | solution.py:41
  148.3 14.3 %collective-permute-start.32 = (bf16[4,3,128,128]{3,2,1,0:T(8,128)(2,1)S(1)}, bf16[4,3,128,128]{3,2,1,0:T(8,128)(2,1)S(1)}, u32[]{:S(2)}, u32[]{:S(2)}) collective-permute-start(bf16[4,3,128,128]{3,2,1,0:T(8,128)(2,1)S(1)} %pad_maximum_fusion.1.refs_1_), channel_id=1, source_target_pairs={{0,64},{32,96},{64,0},{96,32},{1,65},{33,97},{65,1},{97,33},{2,66}... | collective-permute-start | bytes 1179656 | tf_op jit(solution)/shard_map/ppermute | solution.py:41
  151.2 16.9 %collective-permute-start.35 = (bf16[4,3,128,128]{3,2,1,0:T(8,128)(2,1)S(1)}, bf16[4,3,128,128]{3,2,1,0:T(8,128)(2,1)S(1)}, u32[]{:S(2)}, u32[]{:S(2)}) collective-permute-start(bf16[4,3,128,128]{3,2,1,0:T(8,128)(2,1)S(1)} %pad_maximum_fusion.refs_0_), channel_id=1, source_target_pairs={{0,4},{4,0},{1,5},{5,1},{2,6},{6,2},{3,7},{7,3},{8,12},{12,8},{9,1... | collective-permute-start | bytes 1179656 | tf_op jit(solution)/shard_map/ppermute | solution.py:41
  159.0 15.2 %collective-permute-start.37 = (bf16[4,3,128,128]{3,2,1,0:T(8,128)(2,1)S(1)}, bf16[4,3,128,128]{3,2,1,0:T(8,128)(2,1)S(1)}, u32[]{:S(2)}, u32[]{:S(2)}) collective-permute-start(bf16[4,3,128,128]{3,2,1,0:T(8,128)(2,1)S(1)} %pad_maximum_fusion.refs_0_), channel_id=1, source_target_pairs={{0,8},{8,16},{16,24},{24,0},{1,9},{9,17},{17,25},{25,1},{2,10},{10... | collective-permute-start | bytes 1179656 | tf_op jit(solution)/shard_map/ppermute | solution.py:41
  160.6 1.3 collective-permute-start.45
  161.9 13.6 %collective-permute-start.36 = (bf16[4,3,128,128]{3,2,1,0:T(8,128)(2,1)S(1)}, bf16[4,3,128,128]{3,2,1,0:T(8,128)(2,1)S(1)}, u32[]{:S(2)}, u32[]{:S(2)}) collective-permute-start(bf16[4,3,128,128]{3,2,1,0:T(8,128)(2,1)S(1)} %pad_maximum_fusion.1.refs_1_), channel_id=1, source_target_pairs={{0,4},{4,0},{1,5},{5,1},{2,6},{6,2},{3,7},{7,3},{8,12},{12,8},{9,1... | collective-permute-start | bytes 1179656 | tf_op jit(solution)/shard_map/ppermute | solution.py:41
  162.2 13.4 %collective-permute-start.38 = (bf16[4,3,128,128]{3,2,1,0:T(8,128)(2,1)S(1)}, bf16[4,3,128,128]{3,2,1,0:T(8,128)(2,1)S(1)}, u32[]{:S(2)}, u32[]{:S(2)}) collective-permute-start(bf16[4,3,128,128]{3,2,1,0:T(8,128)(2,1)S(1)} %pad_maximum_fusion.1.refs_1_), channel_id=1, source_target_pairs={{0,32},{32,64},{64,96},{96,0},{1,33},{33,65},{65,97},{97,1},{2,34}... | collective-permute-start | bytes 1179656 | tf_op jit(solution)/shard_map/ppermute | solution.py:41
  162.6 13.5 %collective-permute-start.41 = (bf16[4,3,128,128]{3,2,1,0:T(8,128)(2,1)S(1)}, bf16[4,3,128,128]{3,2,1,0:T(8,128)(2,1)}, u32[]{:S(2)}, u32[]{:S(2)}) collective-permute-start(bf16[4,3,128,128]{3,2,1,0:T(8,128)(2,1)S(1)} %pad_maximum_fusion.refs_0_), channel_id=1, source_target_pairs={{0,24},{8,0},{16,8},{24,16},{1,25},{9,1},{17,9},{25,17},{2,26},{10... | collective-permute-start | bytes 1179656 | tf_op jit(solution)/shard_map/ppermute | solution.py:41
  168.1 9.3 %collective-permute-start.42 = (bf16[4,3,128,128]{3,2,1,0:T(8,128)(2,1)S(1)}, bf16[4,3,128,128]{3,2,1,0:T(8,128)(2,1)}, u32[]{:S(2)}, u32[]{:S(2)}) collective-permute-start(bf16[4,3,128,128]{3,2,1,0:T(8,128)(2,1)S(1)} %pad_maximum_fusion.1.refs_1_), channel_id=1, source_target_pairs={{0,96},{32,0},{64,32},{96,64},{1,97},{33,1},{65,33},{97,65},{2,98}... | collective-permute-start | bytes 1179656 | tf_op jit(solution)/shard_map/ppermute | solution.py:41
  174.2 5.5 %collective-permute-start.39 = (bf16[4,3,128,128]{3,2,1,0:T(8,128)(2,1)S(1)}, bf16[4,3,128,128]{3,2,1,0:T(8,128)(2,1)}, u32[]{:S(2)}, u32[]{:S(2)}) collective-permute-start(bf16[4,3,128,128]{3,2,1,0:T(8,128)(2,1)S(1)} %collective-permute-done.37.refs_4_), channel_id=1, source_target_pairs={{0,4},{4,0},{1,5},{5,1},{2,6},{6,2},{3,7},{7,3},{8,12},{12,8},{9,1... | collective-permute-start | bytes 1179656 | tf_op jit(solution)/shard_map/ppermute | solution.py:41
  175.4 15.3 %collective-permute-start.33 = (bf16[4,3,128,128]{3,2,1,0:T(8,128)(2,1)S(1)}, bf16[4,3,128,128]{3,2,1,0:T(8,128)(2,1)S(1)}, u32[]{:S(2)}, u32[]{:S(2)}) collective-permute-start(bf16[4,3,128,128]{3,2,1,0:T(8,128)(2,1)S(1)} %collective-permute-done.22.refs_0_), channel_id=1, source_target_pairs={{0,4},{4,0},{1,5},{5,1},{2,6},{6,2},{3,7},{7,3},{8,12},{12,8},{9,1... | collective-permute-start | bytes 1179656 | tf_op jit(solution)/shard_map/ppermute | solution.py:41
  175.5 15.2 %collective-permute-start.34 = (bf16[4,3,128,128]{3,2,1,0:T(8,128)(2,1)S(1)}, bf16[4,3,128,128]{3,2,1,0:T(8,128)(2,1)S(1)}, u32[]{:S(2)}, u32[]{:S(2)}) collective-permute-start(bf16[4,3,128,128]{3,2,1,0:T(8,128)(2,1)S(1)} %collective-permute-done.32.refs_1_), channel_id=1, source_target_pairs={{0,4},{4,0},{1,5},{5,1},{2,6},{6,2},{3,7},{7,3},{8,12},{12,8},{9,1... | collective-permute-start | bytes 1179656 | tf_op jit(solution)/shard_map/ppermute | solution.py:41
  176.0 6.4 %collective-permute-start.40 = (bf16[4,3,128,128]{3,2,1,0:T(8,128)(2,1)S(1)}, bf16[4,3,128,128]{3,2,1,0:T(8,128)(2,1)S(1)}, u32[]{:S(2)}, u32[]{:S(2)}) collective-permute-start(bf16[4,3,128,128]{3,2,1,0:T(8,128)(2,1)S(1)} %collective-permute-done.38.refs_5_), channel_id=1, source_target_pairs={{0,4},{4,0},{1,5},{5,1},{2,6},{6,2},{3,7},{7,3},{8,12},{12,8},{9,1... | collective-permute-start | bytes 1179656 | tf_op jit(solution)/shard_map/ppermute | solution.py:41
  177.4 5.0 %collective-permute-start.43 = (bf16[4,3,128,128]{3,2,1,0:T(8,128)(2,1)}, bf16[4,3,128,128]{3,2,1,0:T(8,128)(2,1)S(1)}, u32[]{:S(2)}, u32[]{:S(2)}) collective-permute-start(bf16[4,3,128,128]{3,2,1,0:T(8,128)(2,1)} %collective-permute-done.41.refs_8_), channel_id=1, source_target_pairs={{0,4},{4,0},{1,5},{5,1},{2,6},{6,2},{3,7},{7,3},{8,12},{12,8},{9,1... | collective-permute-start | bytes 1179656 | tf_op jit(solution)/shard_map/ppermute | solution.py:41
  179.7 2.7 %collective-permute-start.44 = (bf16[4,3,128,128]{3,2,1,0:T(8,128)(2,1)}, bf16[4,3,128,128]{3,2,1,0:T(8,128)(2,1)S(1)}, u32[]{:S(2)}, u32[]{:S(2)}) collective-permute-start(bf16[4,3,128,128]{3,2,1,0:T(8,128)(2,1)} %collective-permute-done.42.refs_9_), channel_id=1, source_target_pairs={{0,4},{4,0},{1,5},{5,1},{2,6},{6,2},{3,7},{7,3},{8,12},{12,8},{9,1... | collective-permute-start | bytes 1179656 | tf_op jit(solution)/shard_map/ppermute | solution.py:41
  (32 other events, 110.9 us)
